TPU v7x, 32 devices: a whole 2x2x4 slice. The times are simulated.
32 devices in a mesh: ia: 4 (over y, x), ja: 2 (over core), ka: 4 (over z).
Axes of the slice: x: 2, y: 2, z: 4, core: 2. Of those that a mesh axis runs over, the one named last changes fastest.
Arguments:
- tensor: bfloat16 [4096, 32, 4096], P('ia', 'ka', 'ja'), may hold values from -64 to 64
- factor_j: bfloat16 [4096, 128], P('ja'), may hold values from -0.0640625 to 0.0640625
- factor_k: bfloat16 [32, 128], P('ka'), may hold values from -0.72478445 to 0.72478445
Outputs:
- core: float32 [128, 32, 4096], P('ia', 'ka', 'ja')
All inputs are finite; a program needn't handle non-finite values.
Results may differ from a plain program's by a relative error of at most 0.013.
Values may be sent and summed in bfloat16 or wider, within the bound.
A program may use at most 128 MiB of HBM per device.

v0:
```python
import jax
import jax.numpy as jnp
from jax import lax
from jax.sharding import PartitionSpec as P


def local_sketch(tensor, factor_j, factor_k):
    rows, slices, columns = tensor.shape
    mixed = jnp.dot(
        tensor.reshape(rows * slices, columns), factor_j, preferred_element_type=jnp.float32
    )
    mixed = mixed.reshape(rows, slices, factor_j.shape[1])
    return jnp.sum(mixed * factor_k.astype(jnp.float32)[None], axis=1)


def local_gram(basis):
    return jnp.dot(
        basis.T, basis, precision=lax.Precision.HIGHEST, preferred_element_type=jnp.float32
    )


def apply_factor(gram, basis):
    lower = jnp.linalg.cholesky(gram)
    return jax.scipy.linalg.solve_triangular(lower, basis.T, lower=True).T


def shards(tensor, factor_j, factor_k):
    rows, slices, columns = tensor.shape
    partial_value = local_sketch(tensor, factor_j, factor_k)
    basis = lax.psum(partial_value, ("ja", "ka"))
    for sweep in range(2):
        gram = lax.psum(local_gram(basis), "ia")
        basis = apply_factor(gram, basis)
    basis_half = basis.astype(jnp.bfloat16)
    flattened = tensor.reshape(rows, slices * columns)
    width = basis_half.shape[1]
    kept_rows = width // lax.axis_size("ia")
    core = lax.psum_scatter(
        lax.dot_general(
            basis_half, flattened, (((0,), (0,)), ((), ())), preferred_element_type=jnp.float32
        ).astype(jnp.bfloat16),
        "ia",
        scatter_dimension=0,
        tiled=True,
    ).astype(jnp.float32)
    return core.reshape(kept_rows, slices, columns)


def solution(mesh):
    return jax.shard_map(
        shards,
        mesh=mesh,
        in_specs=(P("ia", "ka", "ja"), P("ja", None), P("ka", None)),
        out_specs=P("ia", "ka", "ja"),
        check_vma=False,
    )
```

profile of v0, /device:TPU:0, one launch (start us, length us, event | category | flops | bytes accessed | tf_op | source)
XLA Modules:
  0.0 300.6 jit_solution(7561206188565948169)
XLA Ops:
  6.5 0.7 convert_element_type.11
  7.3 0.3 copy-done
  7.6 14.7 %fusion.3 = f32[1024,8,128]{2,1,0:T(8,128)S(1)} fusion(bf16[1024,8,2048]{2,1,0:T(8,128)(2,1)} %param.6, bf16[2048,128]{1,0:T(8,128)(2,1)S(1)} %copy-done), kind=kOutput, calls=%fused_computation.6 | convolution fusion | flops 4294967296 | bytes 38273024 | tf_op jit(solution)/shard_map/dot_general | solution.py:9
  22.3 1.4 fusion
  23.7 0.0 all-reduce.4.cloned.1.call-update
  23.7 0.0 all-reduce.6.cloned.1.call-start
  23.8 58.9 %all-reduce.4.cloned.1.call-done = f32[1024,128]{1,0:T(8,128)} async-done(((f32[1024,128]{1,0:T(8,128)}), f32[1024,128]{1,0:T(8,128)}) %all-reduce.4.cloned.1.call-update) | async-done | bytes 524304 | tf_op jit(solution)/shard_map/psum | solution.py:30
  82.7 2.8 fusion.13
  85.6 0.2 all-reduce.8.cloned.1.call-start
  85.8 40.5 %all-reduce.6.cloned.1.call-done = f32[128,128]{0,1:T(8,128)} async-done(((f32[128,128]{0,1:T(8,128)}), f32[128,128]{0,1:T(8,128)}) %all-reduce.6.cloned.1.call-update) | async-done | bytes 65552 | tf_op jit(solution)/shard_map/psum | solution.py:32
  126.3 0.9 copy.6
  127.2 0.9 fusion.10
  128.1 11.7 %cholesky.44 = f32[128,128]{1,0:T(8,128)S(1)} custom-call(f32[128,128]{1,0:T(8,128)S(1)} %fusion.10), custom_call_target="Cholesky" | custom-call | tf_op jit(solution)/shard_map/jit(cholesky)/cholesky | solution.py:23
  139.8 0.6 compare_reduce_fusion.1
  140.5 0.7 fusion.5
  141.2 9.8 %custom-call.6 = f32[1,128,128]{1,2,0:T(8,128)S(1)} custom-call(f32[1,128,128]{2,1,0:T(8,128)S(1)} %fusion.5), custom_call_target="InvertDiagBlocksLowerTriangular" | custom-call | tf_op jit(solution)/shard_map/jit(_solve_triangular)/triangular_solve | solution.py:24
  151.0 1.7 fusion.1
  152.7 1.2 fusion.14
  153.9 0.0 all-reduce.8.cloned.1.call-update
  153.9 0.0 reduce-scatter.2.cloned.1.call-start
  154.0 30.1 %copy.13 = bf16[128,8,8,2048]{3,1,2,0:T(8,128)(2,1)} copy(bf16[128,8,8,2048]{3,2,1,0:T(8,128)(2,1)} %bitcast.37) | data formatting | bytes 67108864
  184.0 11.5 %all-reduce.8.cloned.1.call-done = f32[128,128]{0,1:T(8,128)} async-done(((f32[128,128]{0,1:T(8,128)}), f32[128,128]{0,1:T(8,128)}) %all-reduce.8.cloned.1.call-update) | async-done | bytes 65552 | tf_op jit(solution)/shard_map/psum | solution.py:32
  195.6 0.9 copy.8
  196.5 0.9 fusion.8
  197.3 11.7 %cholesky.55 = f32[128,128]{1,0:T(8,128)S(1)} custom-call(f32[128,128]{1,0:T(8,128)S(1)} %fusion.8), custom_call_target="Cholesky" | custom-call | tf_op jit(solution)/shard_map/jit(cholesky)/cholesky | solution.py:23
  209.1 0.6 compare_reduce_fusion
  209.7 0.7 fusion.6
  210.4 9.8 %custom-call.7 = f32[1,128,128]{1,2,0:T(8,128)S(1)} custom-call(f32[1,128,128]{2,1,0:T(8,128)S(1)} %fusion.6), custom_call_target="InvertDiagBlocksLowerTriangular" | custom-call | tf_op jit(solution)/shard_map/jit(_solve_triangular)/triangular_solve | solution.py:24
  220.2 0.6 convolution_convert_fusion.1
  220.9 17.2 %convolution_convert_fusion = bf16[128,16384]{1,0:T(8,128)(2,1)} fusion(bf16[128,1024]{1,0:T(8,128)(2,1)S(1)} %convolution_convert_fusion.1, bf16[1024,16384]{1,0:T(8,128)(2,1)} %bitcast.38), kind=kOutput, calls=%fused_computation | convolution fusion | flops 4297064448 | bytes 38010880 | tf_op jit(solution)/shard_map/dot_general | solution.py:39
  238.1 52.9 %reduce-scatter.2.cloned.1.call-done = bf16[32,16384]{1,0:T(8,128)(2,1)} async-done(((bf16[128,16384]{1,0:T(8,128)(2,1)}), bf16[32,16384]{1,0:T(8,128)(2,1)}) %reduce-scatter.2.cloned.1.call-update) | async-done | bytes 1048592 | tf_op jit(solution)/shard_map/reduce_scatter | solution.py:38
  290.9 3.2 %copy.14 = f32[4,8,8,2048]{3,2,1,0:T(8,128)} copy(bf16[4,8,8,2048]{3,1,2,0:T(8,128)(2,1)} %bitcast.39) | data formatting | bytes 3145728
  (8 shorter events, 0.1 us)
Async XLA Ops:
  6.5 1.1 copy-start
  6.5 76.2 %all-reduce.4.cloned.1.call-start = ((), (), s32[]{:S(2)}) async-start(), calls=%async_computation.1 | async-start | bytes 1048576 | tf_op jit(solution)/shard_map/psum | solution.py:30
  23.7 102.6 %all-reduce.6.cloned.1.call-start = ((), (), s32[]{:S(2)}) async-start(), calls=%async_computation.2 | async-start | bytes 131072 | tf_op jit(solution)/shard_map/psum | solution.py:32
  85.6 110.0 %all-reduce.8.cloned.1.call-start = ((), (), s32[]{:S(2)}) async-start(), calls=%async_computation.3 | async-start | bytes 131072 | tf_op jit(solution)/shard_map/psum | solution.py:32
  153.9 137.0 %reduce-scatter.2.cloned.1.call-start = ((), (), s32[]{:S(2)}) async-start(), calls=%async_computation.4 | async-start | bytes 5242880 | tf_op jit(solution)/shard_map/reduce_scatter | solution.py:38
  220.8 73.3 %copy-start.1 = (bf16[2048,128]{1,0:T(8,128)(2,1)S(1)}, bf16[2048,128]{1,0:T(8,128)(2,1)}, u32[]{:S(2)}) copy-start(bf16[2048,128]{1,0:T(8,128)(2,1)} %param.7) | copy-start | bytes 1572868
Sparse Core Ops, SparseCore 0:
  23.8 58.8 all-reduce.3
  85.8 40.4 all-reduce.5
  154.0 41.4 all-reduce.7
  238.2 52.6 reduce-scatter.1
where the time goes:
time: 301 us
  waiting for transfers between devices  164 us (54%)
  other arithmetic  49.5 us (16%)
  matrix products  38.2 us (13%)
  local copies, waits for them, and re-layouts  35.4 us (12%)
  between operations  13.2 us (4%)
    psum x1, waiting for transfers between devices, shards(): basis = lax.psum(partial_value, ('ja', 'ka'))  58.9 us
    reduce_scatter x1, waiting for transfers between devices, shards(): lax.psum_scatter(lax.dot_general(basis_half, flattened, (((0,), (0,)), ((...  52.9 us
    psum x2, waiting for transfers between devices, shards(): gram = lax.psum(local_gram(basis), 'ia')  52.1 us
    unnamed x6, local copies, waits for them, and re-layouts  33.5 us
    another operation x6, other arithmetic, apply_factor(): lower = jnp.linalg.cholesky(gram)  24.8 us
    another operation x4, other arithmetic, apply_factor(): return jax.scipy.linalg.solve_triangular(lower, basis.T, lower=True).T  20.9 us
    dot_general x1, matrix products, shards(): lax.dot_general(basis_half, flattened, (((0,), (0,)), ((), ())), preferre...  17.2 us
    dot_general x1, matrix products, local_sketch(): jnp.dot(tensor.reshape(rows * slices, columns), factor_j, preferred_eleme...  14.7 us
  transfers between devices with their start and end apart: 4, of which 4 were waited for; matrix products, arithmetic and copies ran while one was open for 10% of the time, Pallas kernels for 0%

commit v1 on v0

v1 whole, which is shorter than its diff:
```python
import functools

import jax
import jax.numpy as jnp
from jax import lax
from jax.experimental import pallas as pl
from jax.experimental.pallas import tpu as pltpu
from jax.sharding import PartitionSpec as P

MESH = pl.DeviceIdType.MESH
F32 = jnp.float32
BF16 = jnp.bfloat16
HIGHEST = lax.Precision.HIGHEST
MIB = 1024 * 1024


def greet(targets):
    barrier = pltpu.get_barrier_semaphore()
    for target in targets:
        pl.semaphore_signal(barrier, inc=1, device_id=target, device_id_type=MESH)
    pl.semaphore_wait(barrier, len(targets))


def sketch_kernel(
    depth, slices, t_ref, fj_ref, fk_ref, out_ref,
    tiles, parts, from_core, from_z, whole,
    load_sems, core_send, core_recv, z_send, z_recv, gz_send, gz_recv, gc_send, gc_recv,
):
    rows = out_ref.shape[0]
    width = out_ref.shape[1]
    share = rows // (2 * depth)
    z, core = lax.axis_index("ka"), lax.axis_index("ja")
    partner = {"ja": 1 - core}
    peers = [lax.rem(z + 1 + s, depth) for s in range(depth - 1)]
    order = [(lax.rem(z + 1 + s, depth), side) for s in range(depth) for side in (1, 0)]

    def offset(owner_z, owner_core):
        return pl.multiple_of((owner_z * 2 + owner_core) * share, share)

    def load(step):
        owner_z, side = order[step]
        owner_core = 1 - core if side else core
        start = pl.multiple_of((owner_z * 2 + owner_core) * share * slices, share * slices)
        return pltpu.make_async_copy(
            t_ref.at[pl.ds(start, share * slices)], tiles.at[step % 3], load_sems.at[step % 3]
        )

    load(0).start()
    load(1).start()
    greet([partner] + [{"ka": peer} for peer in peers])
    weights = fk_ref[...].astype(F32)
    block = min(share, 32)
    core_copies, z_copies = [], []
    for step in range(2 * depth):
        if step + 2 < 2 * depth:
            load(step + 2).start()
        load(step).wait()
        slot = step % 3

        @pl.loop(0, share // block)
        def _(index):
            lines = pl.ds(pl.multiple_of(index * block * slices, block * slices), block * slices)
            mixed = jnp.dot(tiles[slot, lines, :], fj_ref[...], preferred_element_type=F32)
            mixed = mixed.reshape(block, slices, width) * weights[None]
            parts[step, pl.ds(pl.multiple_of(index * block, block), block), :] = jnp.sum(mixed, axis=1)

        hop = step // 2
        if step % 2 == 0:
            copy = pltpu.make_async_remote_copy(
                parts.at[step], from_core.at[hop], core_send.at[hop], core_recv.at[hop],
                device_id=partner, device_id_type=MESH,
            )
            copy.start()
            core_copies.append(copy)
        else:
            core_copies[hop].wait_recv()
            parts[step] = parts[step] + from_core[hop]
            if hop < depth - 1:
                copy = pltpu.make_async_remote_copy(
                    parts.at[step], from_z.at[hop], z_send.at[hop], z_recv.at[hop],
                    device_id={"ka": order[step][0]}, device_id_type=MESH,
                )
                copy.start()
                z_copies.append(copy)

    total = parts[2 * depth - 1]
    for copy, slot in zip(z_copies, range(depth - 1)):
        copy.wait_recv()
        total = total + from_z[slot]
    mine = pl.ds(offset(z, core), share)
    whole[mine, :] = total
    gz = []
    for s, peer in enumerate(peers):
        copy = pltpu.make_async_remote_copy(
            whole.at[mine], whole.at[mine], gz_send.at[s], gz_recv.at[s],
            device_id={"ka": peer}, device_id_type=MESH,
        )
        copy.start()
        gz.append(copy)

    def to_partner(owner, index):
        lines = pl.ds(offset(owner, core), share)
        copy = pltpu.make_async_remote_copy(
            whole.at[lines], whole.at[lines], gc_send.at[index], gc_recv.at[index],
            device_id=partner, device_id_type=MESH,
        )
        copy.start()
        return copy

    gc = [to_partner(z, 0)]
    for s in range(depth - 1):
        gz[s].wait_recv()
        gc.append(to_partner(lax.rem(z + depth - 1 - s, depth), 1 + s))
    for copy in gc:
        copy.wait_recv()
    for copy in core_copies + z_copies + gz + gc:
        copy.wait_send()
    out_ref[...] = whole[...]


def sketch_sum(tensor, factor_j, factor_k, depth):
    rows, slices, columns = tensor.shape
    width = factor_j.shape[1]
    share = rows // (2 * depth)
    dma = lambda n: pltpu.SemaphoreType.DMA((n,))
    return pl.pallas_call(
        functools.partial(sketch_kernel, depth, slices),
        out_shape=jax.ShapeDtypeStruct((rows, width), F32),
        in_specs=[pl.BlockSpec(memory_space=pl.ANY)] + [pl.BlockSpec(memory_space=pltpu.VMEM)] * 2,
        out_specs=pl.BlockSpec(memory_space=pltpu.VMEM),
        scratch_shapes=[
            pltpu.VMEM((3, share * slices, columns), BF16),
            pltpu.VMEM((2 * depth, share, width), F32),
            pltpu.VMEM((depth, share, width), F32),
            pltpu.VMEM((depth, share, width), F32),
            pltpu.VMEM((rows, width), F32),
            dma(3), dma(depth), dma(depth), dma(depth), dma(depth),
            dma(depth), dma(depth), dma(depth), dma(depth),
        ],
        compiler_params=pltpu.CompilerParams(
            collective_id=0, has_side_effects=True, vmem_limit_bytes=40 * MIB
        ),
        cost_estimate=pl.CostEstimate(
            flops=2 * rows * slices * columns * width,
            bytes_accessed=2 * rows * slices * columns, transcendentals=0,
        ),
    )(tensor.reshape(rows * slices, columns), factor_j, factor_k)


def gram_kernel(count, rows_ref, out_ref, grams, send, recv):
    me = lax.axis_index("ia")
    peers = [lax.rem(me + 1 + s, count) for s in range(count - 1)]
    greet([{"ia": peer} for peer in peers])
    value = rows_ref[...]
    grams[me] = lax.dot_general(
        value, value, (((0,), (0,)), ((), ())), precision=HIGHEST, preferred_element_type=F32
    )
    copies = []
    for s, peer in enumerate(peers):
        copy = pltpu.make_async_remote_copy(
            grams.at[me], grams.at[me], send.at[s], recv.at[s],
            device_id={"ia": peer}, device_id_type=MESH,
        )
        copy.start()
        copies.append(copy)
    for copy in copies:
        copy.wait_recv()
    total = grams[0]
    for index in range(1, count):
        total = total + grams[index]
    out_ref[...] = total
    for copy in copies:
        copy.wait_send()


def gram_sum(value, count):
    width = value.shape[1]
    return pl.pallas_call(
        functools.partial(gram_kernel, count),
        out_shape=jax.ShapeDtypeStruct((width, width), F32),
        in_specs=[pl.BlockSpec(memory_space=pltpu.VMEM)],
        out_specs=pl.BlockSpec(memory_space=pltpu.VMEM),
        scratch_shapes=[
            pltpu.VMEM((count, width, width), F32),
            pltpu.SemaphoreType.DMA((count,)),
            pltpu.SemaphoreType.DMA((count,)),
        ],
        compiler_params=pltpu.CompilerParams(collective_id=1, has_side_effects=True),
    )(value)


def inverse_factor(gram, work):
    width = gram.shape[0]
    work[:, :width] = gram
    lines = lax.broadcasted_iota(jnp.int32, (width, width), 0)
    lanes = lax.broadcasted_iota(jnp.int32, (width, width), 1)
    work[:, width:] = jnp.where(lines == lanes, 1.0, 0.0).astype(F32)
    for first in range(0, width, 8):
        panel = work[first:first + 8, :]
        rows = [panel[k:k + 1, :] for k in range(8)]
        cells = {}
        for k in range(8):
            for i in range(k, 8):
                cells[k, i] = jnp.broadcast_to(
                    panel[k:k + 1, first + i:first + i + 1], (1, 2 * width)
                )
        for k in range(8):
            scale = lax.rsqrt(cells[k, k])
            rows[k] = rows[k] * scale
            lower = [None] * 8
            for i in range(k + 1, 8):
                lower[i] = cells[k, i] * scale
            for i in range(k + 1, 8):
                rows[i] = rows[i] - lower[i] * rows[k]
                for m in range(i, 8):
                    cells[i, m] = cells[i, m] - lower[i] * lower[m]
        done = jnp.concatenate(rows, axis=0)
        work[first:first + 8, :] = done
        if first + 8 < width:
            work[first + 8:, :] = work[first + 8:, :] - lax.dot_general(
                done[:, :width], done, (((0,), (0,)), ((), ())),
                precision=HIGHEST, preferred_element_type=F32,
            )[first + 8:, :]


def apply_kernel(gram_ref, rows_ref, out_ref, work):
    width = gram_ref.shape[0]
    inverse_factor(gram_ref[...], work)
    out_ref[...] = lax.dot_general(
        rows_ref[...], work[:, width:], (((1,), (1,)), ((), ())),
        precision=HIGHEST, preferred_element_type=F32,
    ).astype(out_ref.dtype)


def apply_factor(gram, value, dtype):
    width = gram.shape[0]
    return pl.pallas_call(
        apply_kernel,
        out_shape=jax.ShapeDtypeStruct(value.shape, dtype),
        in_specs=[pl.BlockSpec(memory_space=pltpu.VMEM)] * 2,
        out_specs=pl.BlockSpec(memory_space=pltpu.VMEM),
        scratch_shapes=[pltpu.VMEM((width, 2 * width), F32)],
    )(gram, value)


def project_kernel(count, t_ref, half_ref, out_ref, tiles, parts, landed, load_sems, send, recv):
    rows = half_ref.shape[0]
    width = half_ref.shape[1]
    kept = width // count
    chunk = tiles.shape[2]
    steps = t_ref.shape[1] // chunk
    me = lax.axis_index("ia")
    peers = [lax.rem(me + 1 + s, count) for s in range(count - 1)]
    strip = 512

    def load(step):
        return pltpu.make_async_copy(
            t_ref.at[:, pl.ds(step * chunk, chunk)], tiles.at[step % 2], load_sems.at[step % 2]
        )

    load(0).start()
    greet([{"ia": peer} for peer in peers])
    copies = []
    for step in range(steps):
        if step + 1 < steps:
            load(step + 1).start()
        load(step).wait()

        @pl.loop(0, chunk // strip)
        def _(index):
            cols = pl.ds(pl.multiple_of(index * strip, strip), strip)
            value = lax.dot_general(
                half_ref[...], tiles[step % 2, :, cols], (((0,), (0,)), ((), ())),
                preferred_element_type=F32,
            ).astype(BF16)
            parts[step, :, :, cols] = value.reshape(count, kept, strip)

        for s, peer in enumerate(peers):
            copy = pltpu.make_async_remote_copy(
                parts.at[step, peer], landed.at[step, s], send.at[step, s], recv.at[step, s],
                device_id={"ia": peer}, device_id_type=MESH,
            )
            copy.start()
            copies.append(copy)
    for step in range(steps):
        for s in range(count - 1):
            copies[step * (count - 1) + s].wait_recv()
        total = parts[step, me].astype(F32)
        for s in range(count - 1):
            total = total + landed[step, s].astype(F32)
        out_ref[:, pl.ds(step * chunk, chunk)] = total
    for copy in copies:
        copy.wait_send()


def project(flat, half, count):
    rows, columns = flat.shape
    width = half.shape[1]
    kept = width // count
    chunk = 2048
    steps = columns // chunk
    return pl.pallas_call(
        functools.partial(project_kernel, count),
        out_shape=jax.ShapeDtypeStruct((kept, columns), F32),
        in_specs=[pl.BlockSpec(memory_space=pl.ANY), pl.BlockSpec(memory_space=pltpu.VMEM)],
        out_specs=pl.BlockSpec(memory_space=pltpu.VMEM),
        scratch_shapes=[
            pltpu.VMEM((2, rows, chunk), BF16),
            pltpu.VMEM((steps, count, kept, chunk), BF16),
            pltpu.VMEM((steps, count, kept, chunk), BF16),
            pltpu.SemaphoreType.DMA((2,)),
            pltpu.SemaphoreType.DMA((steps, count)),
            pltpu.SemaphoreType.DMA((steps, count)),
        ],
        compiler_params=pltpu.CompilerParams(
            collective_id=2, has_side_effects=True, vmem_limit_bytes=48 * MIB
        ),
        cost_estimate=pl.CostEstimate(
            flops=2 * rows * columns * width, bytes_accessed=2 * rows * columns, transcendentals=0,
        ),
    )(flat, half)


def shards(tensor, factor_j, factor_k):
    rows, slices, columns = tensor.shape
    count, depth = lax.axis_size("ia"), lax.axis_size("ka")
    sketch = sketch_sum(tensor, factor_j, factor_k, depth)
    basis = apply_factor(gram_sum(sketch, count), sketch, F32)
    half = apply_factor(gram_sum(basis, count), basis, BF16)
    core = project(tensor.reshape(rows, slices * columns), half, count)
    return core.reshape(core.shape[0], slices, columns)


def solution(mesh):
    return jax.shard_map(
        shards,
        mesh=mesh,
        in_specs=(P("ia", "ka", "ja"), P("ja", None), P("ka", None)),
        out_specs=P("ia", "ka", "ja"),
        check_vma=False,
    )
```

time: 301 us -> 152 us (0.50)
  waiting for transfers between devices: 164 us -> 0 us
  Pallas kernels: 0 us -> 116 us
  other arithmetic: 49.5 us -> 0 us
  matrix products: 38.2 us -> 0 us
  between operations: 13.2 us -> 0.05 us
    pallas_call x0 -> x6, Pallas kernels: none -> 116 us  [the longest x1 49.9 us: project(): pl.pallas_call(functools.partial(project_kernel, count), out_shape=jax.Sh...]
    psum x3 -> x0, waiting for transfers between devices: 111 us -> none  [the longest x1 58.9 us: shards(): basis = lax.psum(partial_value, ('ja', 'ka'))]
    reduce_scatter x1 -> x0, waiting for transfers between devices: 52.9 us -> none  [shards(): lax.psum_scatter(lax.dot_general(basis_half, flattened, (((0,), (0,)), ((...]
    another operation x10 -> x0, other arithmetic: 45.7 us -> none  [the longest x6 24.8 us: apply_factor(): lower = jnp.linalg.cholesky(gram)]
    dot_general x4 -> x0, matrix products: 35.9 us -> none  [the longest x1 17.2 us: shards(): lax.dot_general(basis_half, flattened, (((0,), (0,)), ((), ())), preferre...]
    unnamed x6 -> x10, local copies, waits for them, and re-layouts: 33.5 us -> 35.3 us
  transfers between devices with their start and end apart: 4 -> 0, of which waited for: 4 -> 0; matrix products, arithmetic and copies ran while one was open for 10% -> 0% of each run, Pallas kernels for 0% -> 0%
where the time goes in v1:
time: 152 us; the launch traced here: 151 us
  Pallas kernels  116 us (76%)
  local copies, waits for them, and re-layouts  35.3 us (23%)
    pallas_call x1, Pallas kernels, project(): pl.pallas_call(functools.partial(project_kernel, count), out_shape=jax.Sh...  49.9 us
    unnamed x10, local copies, waits for them, and re-layouts  35.3 us
    pallas_call x1, Pallas kernels, sketch_sum(): pl.pallas_call(functools.partial(sketch_kernel, depth, slices), out_shape...  27.2 us
    pallas_call x2, Pallas kernels, apply_factor(): pl.pallas_call(apply_kernel, out_shape=jax.ShapeDtypeStruct(value.shape,...  20.8 us
    pallas_call x2, Pallas kernels, gram_sum(): pl.pallas_call(functools.partial(gram_kernel, count), out_shape=jax.Shape...  17.8 us

profile of v1, /device:TPU:0, one launch (start us, length us, event | category | flops | bytes accessed | tf_op | source)
XLA Modules:
  0.0 151.1 jit_solution(14104546388546033753)
XLA Ops:
  0.0 0.0 copy-start.2
  0.0 1.0 copy-done.2
  1.0 0.0 copy-start.3
  1.0 0.7 copy-done.3
  1.7 27.2 %shard_map.37.rows_ref = f32[1024,128]{1,0:T(8,128)S(1)} custom-call(bf16[8192,2048]{1,0:T(8,128)(2,1)} %bitcast.6, bf16[2048,128]{1,0:T(8,128)(2,1)S(1)} %copy-done.2, bf16[8,128]{1,0:T(8,128)(2,1)S(1)} %copy-done.3), custom_call_target="tpu_custom_call" | custom-call | flops 4294967296 | bytes 33554432 | tf_op jit(solution)/shard_map/pallas_call | solution.py:126
  29.0 0.0 copy-start
  29.0 0.8 copy-done
  29.7 9.2 %shard_map.38.gram_ref = f32[128,128]{1,0:T(8,128)} custom-call(f32[1024,128]{1,0:T(8,128)} %copy-done), custom_call_target="tpu_custom_call" | custom-call | tf_op jit(solution)/shard_map/pallas_call | solution.py:178
  38.9 10.5 %shard_map.39.rows_ref = f32[1024,128]{1,0:T(8,128)} custom-call(f32[128,128]{1,0:T(8,128)} %shard_map.38.gram_ref, f32[1024,128]{1,0:T(8,128)} %copy-done), custom_call_target="tpu_custom_call" | custom-call | tf_op jit(solution)/shard_map/pallas_call | solution.py:237
  49.4 8.7 %shard_map.40.gram_ref = f32[128,128]{1,0:T(8,128)} custom-call(f32[1024,128]{1,0:T(8,128)} %shard_map.39.rows_ref), custom_call_target="tpu_custom_call" | custom-call | tf_op jit(solution)/shard_map/pallas_call | solution.py:178
  58.1 10.4 %shard_map.41.half_ref = bf16[1024,128]{1,0:T(8,128)(2,1)} custom-call(f32[128,128]{1,0:T(8,128)} %shard_map.40.gram_ref, f32[1024,128]{1,0:T(8,128)} %shard_map.39.rows_ref), custom_call_target="tpu_custom_call" | custom-call | tf_op jit(solution)/shard_map/pallas_call | solution.py:237
  68.4 0.0 copy-start.1
  68.4 30.3 %copy.4 = bf16[128,8,8,2048]{3,1,2,0:T(8,128)(2,1)} copy(bf16[128,8,8,2048]{3,2,1,0:T(8,128)(2,1)} %bitcast.7) | data formatting | bytes 67108864
  98.7 0.0 copy-done.1
  98.7 49.9 %shard_map.42 = f32[32,16384]{1,0:T(8,128)S(1)} custom-call(bf16[1024,16384]{1,0:T(8,128)(2,1)} %bitcast.8, bf16[1024,128]{1,0:T(8,128)(2,1)S(1)} %copy-done.1), custom_call_target="tpu_custom_call" | custom-call | flops 4294967296 | bytes 33554432 | tf_op jit(solution)/shard_map/pallas_call | solution.py:302
  148.6 2.5 %copy.5 = f32[4,8,8,2048]{3,2,1,0:T(8,128)} copy(f32[4,8,8,2048]{3,1,2,0:T(8,128)S(1)} %bitcast.5) | data formatting | bytes 4194304
Async XLA Ops:
  0.0 1.0 copy-start.2
  1.0 0.7 copy-start.3
  29.0 0.8 copy-start
  68.4 30.3 %copy-start.1 = (bf16[1024,128]{1,0:T(8,128)(2,1)S(1)}, bf16[1024,128]{1,0:T(8,128)(2,1)}, u32[]{:S(2)}) copy-start(bf16[1024,128]{1,0:T(8,128)(2,1)} %shard_map.41.half_ref) | copy-start | bytes 786436

commit v2 on v1

--- a/solution.py
+++ b/solution.py
@@ -223,91 +223,143 @@
             )[first + 8:, :]
 
 
-def apply_kernel(gram_ref, rows_ref, out_ref, work):
+def apply_kernel(flip, gram_ref, rows_ref, out_ref, work):
     width = gram_ref.shape[0]
     inverse_factor(gram_ref[...], work)
+    left, right = rows_ref[...], work[:, width:]
+    if flip:
+        left, right = right, left
     out_ref[...] = lax.dot_general(
-        rows_ref[...], work[:, width:], (((1,), (1,)), ((), ())),
-        precision=HIGHEST, preferred_element_type=F32,
+        left, right, (((1,), (1,)), ((), ())), precision=HIGHEST, preferred_element_type=F32
     ).astype(out_ref.dtype)
 
 
-def apply_factor(gram, value, dtype):
+def apply_factor(gram, value, flip, dtype):
     width = gram.shape[0]
     return pl.pallas_call(
-        apply_kernel,
-        out_shape=jax.ShapeDtypeStruct(value.shape, dtype),
+        functools.partial(apply_kernel, flip),
+        out_shape=jax.ShapeDtypeStruct(value.shape[::-1] if flip else value.shape, dtype),
         in_specs=[pl.BlockSpec(memory_space=pltpu.VMEM)] * 2,
         out_specs=pl.BlockSpec(memory_space=pltpu.VMEM),
         scratch_shapes=[pltpu.VMEM((width, 2 * width), F32)],
     )(gram, value)
 
 
-def project_kernel(count, t_ref, half_ref, out_ref, tiles, parts, landed, load_sems, send, recv):
-    rows = half_ref.shape[0]
-    width = half_ref.shape[1]
-    kept = width // count
-    chunk = tiles.shape[2]
-    steps = t_ref.shape[1] // chunk
+def project_kernel(
+    count, t_ref, half_ref, out_ref, tiles, perm, turned, parts, landed, load_sems, send, recv
+):
+    rows = half_ref.shape[1]
+    kept, slices, columns = out_ref.shape
+    strip = tiles.shape[2]
+    steps = columns // strip
+    group = perm.shape[0] // slices
     me = lax.axis_index("ia")
-    peers = [lax.rem(me + 1 + s, count) for s in range(count - 1)]
-    strip = 512
+    if count == 4:
+        x, y = lax.rem(me, 2), me // 2
+        x_near, y_near, far = me + 1 - 2 * x, me + 2 - 4 * y, 3 - me
+        peers = [x_near, y_near]
+    else:
+        peers = [lax.rem(me + 1 + s, count) for s in range(count - 1)]
 
     def load(step):
         return pltpu.make_async_copy(
-            t_ref.at[:, pl.ds(step * chunk, chunk)], tiles.at[step % 2], load_sems.at[step % 2]
-        )
+            t_ref.at[:, pl.ds(step * strip, strip)], tiles.at[step % 2], load_sems.at[step % 2]
+        )
+
+    def push(source, step, slot, target):
+        copy = pltpu.make_async_remote_copy(
+            parts.at[step, source], landed.at[step, slot], send.at[step, slot], recv.at[step, slot],
+            device_id={"ia": target}, device_id_type=MESH,
+        )
+        copy.start()
+        return copy
 
     load(0).start()
+    line = lax.broadcasted_iota(jnp.int32, perm.shape, 0)
+    lane = lax.broadcasted_iota(jnp.int32, perm.shape, 1)
+    perm[...] = jnp.where(
+        lane == lax.rem(line, group) * slices + lax.div(line, group), 1.0, 0.0
+    ).astype(BF16)
     greet([{"ia": peer} for peer in peers])
-    copies = []
+    copies = {}
+
+    def near(step):
+        return (x_near, y_near) if step % 2 == 0 else (y_near, x_near)
+
+    def relay(step):
+        second = near(step)[1]
+        copies[step, 1].wait_recv()
+        added = parts[step, second].astype(F32) + landed[step, 1].astype(F32)
+        parts[step, second] = added.astype(BF16)
+        copies[step, 2] = push(second, step, 2, second)
+
+    def finish(step):
+        slots = (0, 2) if count == 4 else range(count - 1)
+        total = parts[step, me].astype(F32)
+        for slot in slots:
+            copies[step, slot].wait_recv()
+            total = total + landed[step, slot].astype(F32)
+        for k in range(slices):
+            out_ref[:, k, pl.ds(step * strip, strip)] = total[:, k * strip:(k + 1) * strip]
+
     for step in range(steps):
         if step + 1 < steps:
             load(step + 1).start()
         load(step).wait()
 
-        @pl.loop(0, chunk // strip)
+        @pl.loop(0, rows // group, unroll=4)
         def _(index):
-            cols = pl.ds(pl.multiple_of(index * strip, strip), strip)
-            value = lax.dot_general(
-                half_ref[...], tiles[step % 2, :, cols], (((0,), (0,)), ((), ())),
-                preferred_element_type=F32,
-            ).astype(BF16)
+            span = group * slices
+            lines = pl.ds(pl.multiple_of(index * span, span), span)
+            value = jnp.dot(perm[...], tiles[step % 2, lines, :], preferred_element_type=F32)
+            value = value.astype(BF16)
+            for k in range(slices):
+                place = pl.ds(pl.multiple_of(index * group, group), group)
+                turned[k, place, :] = value[k * group:(k + 1) * group]
+
+        @pl.loop(0, slices, unroll=2)
+        def _(k):
+            value = jnp.dot(half_ref[...], turned[k], preferred_element_type=F32).astype(BF16)
+            cols = pl.ds(pl.multiple_of(k * strip, strip), strip)
             parts[step, :, :, cols] = value.reshape(count, kept, strip)
 
-        for s, peer in enumerate(peers):
-            copy = pltpu.make_async_remote_copy(
-                parts.at[step, peer], landed.at[step, s], send.at[step, s], recv.at[step, s],
-                device_id={"ia": peer}, device_id_type=MESH,
-            )
-            copy.start()
-            copies.append(copy)
-    for step in range(steps):
-        for s in range(count - 1):
-            copies[step * (count - 1) + s].wait_recv()
-        total = parts[step, me].astype(F32)
-        for s in range(count - 1):
-            total = total + landed[step, s].astype(F32)
-        out_ref[:, pl.ds(step * chunk, chunk)] = total
-    for copy in copies:
+        if count == 4:
+            first = near(step)[0]
+            copies[step, 1] = push(far, step, 1, first)
+            copies[step, 0] = push(first, step, 0, first)
+            if step >= 1:
+                relay(step - 1)
+        else:
+            for s, peer in enumerate(peers):
+                copies[step, s] = push(peer, step, s, peer)
+        if step >= 4:
+            finish(step - 4)
+    if count == 4:
+        relay(steps - 1)
+    for step in range(max(steps - 4, 0), steps):
+        finish(step)
+    for copy in copies.values():
         copy.wait_send()
 
 
-def project(flat, half, count):
-    rows, columns = flat.shape
-    width = half.shape[1]
+def project(tensor, half, count):
+    rows, slices, columns = tensor.shape
+    width = half.shape[0]
     kept = width // count
-    chunk = 2048
-    steps = columns // chunk
+    strip = 256
+    steps = columns // strip
+    group = max(256 // slices, 16)
     return pl.pallas_call(
         functools.partial(project_kernel, count),
-        out_shape=jax.ShapeDtypeStruct((kept, columns), F32),
+        out_shape=jax.ShapeDtypeStruct((kept, slices, columns), F32),
         in_specs=[pl.BlockSpec(memory_space=pl.ANY), pl.BlockSpec(memory_space=pltpu.VMEM)],
         out_specs=pl.BlockSpec(memory_space=pltpu.VMEM),
         scratch_shapes=[
-            pltpu.VMEM((2, rows, chunk), BF16),
-            pltpu.VMEM((steps, count, kept, chunk), BF16),
-            pltpu.VMEM((steps, count, kept, chunk), BF16),
+            pltpu.VMEM((2, rows * slices, strip), BF16),
+            pltpu.VMEM((group * slices, group * slices), BF16),
+            pltpu.VMEM((slices, rows, strip), BF16),
+            pltpu.VMEM((steps, count, kept, slices * strip), BF16),
+            pltpu.VMEM((steps, count, kept, slices * strip), BF16),
             pltpu.SemaphoreType.DMA((2,)),
             pltpu.SemaphoreType.DMA((steps, count)),
             pltpu.SemaphoreType.DMA((steps, count)),
@@ -316,19 +368,18 @@
             collective_id=2, has_side_effects=True, vmem_limit_bytes=48 * MIB
         ),
         cost_estimate=pl.CostEstimate(
-            flops=2 * rows * columns * width, bytes_accessed=2 * rows * columns, transcendentals=0,
+            flops=2 * rows * slices * columns * width,
+            bytes_accessed=2 * rows * slices * columns, transcendentals=0,
         ),
-    )(flat, half)
+    )(tensor.reshape(rows * slices, columns), half)
 
 
 def shards(tensor, factor_j, factor_k):
-    rows, slices, columns = tensor.shape
     count, depth = lax.axis_size("ia"), lax.axis_size("ka")
     sketch = sketch_sum(tensor, factor_j, factor_k, depth)
-    basis = apply_factor(gram_sum(sketch, count), sketch, F32)
-    half = apply_factor(gram_sum(basis, count), basis, BF16)
-    core = project(tensor.reshape(rows, slices * columns), half, count)
-    return core.reshape(core.shape[0], slices, columns)
+    basis = apply_factor(gram_sum(sketch, count), sketch, False, F32)
+    half = apply_factor(gram_sum(basis, count), basis, True, BF16)
+    return project(tensor, half, count)
 
 
 def solution(mesh):

time: 152 us -> 117 us (0.77)
  local copies, waits for them, and re-layouts: 35.3 us -> 4.78 us
  Pallas kernels: 116 us -> 112 us
    unnamed x10 -> x9, local copies, waits for them, and re-layouts: 35.3 us -> 4.78 us
    pallas_call x1, Pallas kernels: 49.9 us -> 46.2 us  [project(): pl.pallas_call(functools.partial(project_kernel, count), out_shape=jax.Sh...]
where the time goes in v2:
time: 117 us
  Pallas kernels  112 us (96%)
  local copies, waits for them, and re-layouts  4.78 us (4%)
    pallas_call x1, Pallas kernels, project(): pl.pallas_call(functools.partial(project_kernel, count), out_shape=jax.Sh...  46.2 us
    pallas_call x1, Pallas kernels, sketch_sum(): pl.pallas_call(functools.partial(sketch_kernel, depth, slices), out_shape...  27.2 us
    pallas_call x2, Pallas kernels, apply_factor(): pl.pallas_call(functools.partial(apply_kernel, flip), out_shape=jax.Shape...  20.6 us
    pallas_call x2, Pallas kernels, gram_sum(): pl.pallas_call(functools.partial(gram_kernel, count), out_shape=jax.Shape...  17.8 us
    unnamed x9, local copies, waits for them, and re-layouts  4.78 us

profile of v2, /device:TPU:0, one launch (start us, length us, event | category | flops | bytes accessed | tf_op | source)
XLA Modules:
  0.0 116.7 jit_solution(6056791678330244098)
XLA Ops:
  0.0 0.0 copy-start.2
  0.0 1.0 copy-done.2
  1.0 0.0 copy-start.3
  1.0 0.7 copy-done.3
  1.7 27.2 %shard_map.37.rows_ref = f32[1024,128]{1,0:T(8,128)S(1)} custom-call(bf16[8192,2048]{1,0:T(8,128)(2,1)} %bitcast.1, bf16[2048,128]{1,0:T(8,128)(2,1)S(1)} %copy-done.2, bf16[8,128]{1,0:T(8,128)(2,1)S(1)} %copy-done.3), custom_call_target="tpu_custom_call" | custom-call | flops 4294967296 | bytes 33554432 | tf_op jit(solution)/shard_map/pallas_call | solution.py:126
  29.0 0.0 copy-start
  29.0 0.8 copy-done
  29.7 9.2 %shard_map.38.gram_ref = f32[128,128]{1,0:T(8,128)} custom-call(f32[1024,128]{1,0:T(8,128)} %copy-done), custom_call_target="tpu_custom_call" | custom-call | tf_op jit(solution)/shard_map/pallas_call | solution.py:178
  38.9 10.5 %shard_map.39.rows_ref = f32[1024,128]{1,0:T(8,128)} custom-call(f32[128,128]{1,0:T(8,128)} %shard_map.38.gram_ref, f32[1024,128]{1,0:T(8,128)} %copy-done), custom_call_target="tpu_custom_call" | custom-call | tf_op jit(solution)/shard_map/pallas_call | solution.py:239
  49.4 8.7 %shard_map.40.gram_ref = f32[128,128]{1,0:T(8,128)} custom-call(f32[1024,128]{1,0:T(8,128)} %shard_map.39.rows_ref), custom_call_target="tpu_custom_call" | custom-call | tf_op jit(solution)/shard_map/pallas_call | solution.py:178
  58.1 10.2 %shard_map.41.half_ref = bf16[128,1024]{1,0:T(8,128)(2,1)} custom-call(f32[128,128]{1,0:T(8,128)} %shard_map.40.gram_ref, f32[1024,128]{1,0:T(8,128)} %shard_map.39.rows_ref), custom_call_target="tpu_custom_call" | custom-call | tf_op jit(solution)/shard_map/pallas_call | solution.py:239
  68.3 0.0 copy-start.1
  68.3 0.9 copy-done.1
  69.2 46.2 %shard_map.42 = f32[32,8,2048]{2,1,0:T(8,128)S(1)} custom-call(bf16[8192,2048]{1,0:T(8,128)(2,1)} %bitcast.2, bf16[128,1024]{1,0:T(8,128)(2,1)S(1)} %copy-done.1), custom_call_target="tpu_custom_call" | custom-call | flops 4294967296 | bytes 33554432 | tf_op jit(solution)/shard_map/pallas_call | solution.py:352
  115.4 1.3 %copy.5 = f32[32,8,2048]{2,1,0:T(8,128)} copy(f32[32,8,2048]{2,1,0:T(8,128)S(1)} %shard_map.42) | data formatting | bytes 4194304
Async XLA Ops:
  0.0 1.0 copy-start.2
  1.0 0.7 copy-start.3
  29.0 0.8 copy-start
  68.3 0.9 copy-start.1

commit v3 on v2

--- a/solution.py
+++ b/solution.py
@@ -22,9 +22,10 @@
 
 
 def sketch_kernel(
-    depth, slices, t_ref, fj_ref, fk_ref, out_ref,
-    tiles, parts, from_core, from_z, whole,
+    count, depth, slices, t_ref, fj_hbm, fk_hbm, out_ref, gram_ref,
+    tiles, fj_ref, fk_ref, parts, from_core, from_z, whole, grams,
     load_sems, core_send, core_recv, z_send, z_recv, gz_send, gz_recv, gc_send, gc_recv,
+    gram_send, gram_recv, factor_sems,
 ):
     rows = out_ref.shape[0]
     width = out_ref.shape[1]
@@ -45,9 +46,17 @@
             t_ref.at[pl.ds(start, share * slices)], tiles.at[step % 3], load_sems.at[step % 3]
         )
 
+    factors = [
+        pltpu.make_async_copy(fj_hbm, fj_ref, factor_sems.at[0]),
+        pltpu.make_async_copy(fk_hbm, fk_ref, factor_sems.at[1]),
+    ]
+    for copy in factors:
+        copy.start()
     load(0).start()
     load(1).start()
-    greet([partner] + [{"ka": peer} for peer in peers])
+    greet([partner] + [{"ka": peer} for peer in peers] + other_rows(count))
+    for copy in factors:
+        copy.wait()
     weights = fk_ref[...].astype(F32)
     block = min(share, 32)
     core_copies, z_copies = [], []
@@ -57,7 +66,7 @@
         load(step).wait()
         slot = step % 3
 
-        @pl.loop(0, share // block)
+        @pl.loop(0, share // block, unroll=min(share // block, 4))
         def _(index):
             lines = pl.ds(pl.multiple_of(index * block * slices, block * slices), block * slices)
             mixed = jnp.dot(tiles[slot, lines, :], fj_ref[...], preferred_element_type=F32)
@@ -113,29 +122,36 @@
         gc.append(to_partner(lax.rem(z + depth - 1 - s, depth), 1 + s))
     for copy in gc:
         copy.wait_recv()
+    out_ref[...] = whole[...]
+    gram_ref[...] = exchange(whole[...], count, grams, gram_send, gram_recv)
     for copy in core_copies + z_copies + gz + gc:
         copy.wait_send()
-    out_ref[...] = whole[...]
-
-
-def sketch_sum(tensor, factor_j, factor_k, depth):
+
+
+def sketch_sum(tensor, factor_j, factor_k, count, depth):
     rows, slices, columns = tensor.shape
     width = factor_j.shape[1]
     share = rows // (2 * depth)
     dma = lambda n: pltpu.SemaphoreType.DMA((n,))
     return pl.pallas_call(
-        functools.partial(sketch_kernel, depth, slices),
-        out_shape=jax.ShapeDtypeStruct((rows, width), F32),
-        in_specs=[pl.BlockSpec(memory_space=pl.ANY)] + [pl.BlockSpec(memory_space=pltpu.VMEM)] * 2,
-        out_specs=pl.BlockSpec(memory_space=pltpu.VMEM),
+        functools.partial(sketch_kernel, count, depth, slices),
+        out_shape=[
+            jax.ShapeDtypeStruct((rows, width), F32), jax.ShapeDtypeStruct((width, width), F32)
+        ],
+        in_specs=[pl.BlockSpec(memory_space=pl.ANY)] * 3,
+        out_specs=[pl.BlockSpec(memory_space=pltpu.VMEM)] * 2,
         scratch_shapes=[
             pltpu.VMEM((3, share * slices, columns), BF16),
+            pltpu.VMEM(factor_j.shape, BF16),
+            pltpu.VMEM(factor_k.shape, BF16),
             pltpu.VMEM((2 * depth, share, width), F32),
             pltpu.VMEM((depth, share, width), F32),
             pltpu.VMEM((depth, share, width), F32),
             pltpu.VMEM((rows, width), F32),
+            pltpu.VMEM((count, width, width), F32),
             dma(3), dma(depth), dma(depth), dma(depth), dma(depth),
             dma(depth), dma(depth), dma(depth), dma(depth),
+            dma(count), dma(count), dma(2),
         ],
         compiler_params=pltpu.CompilerParams(
             collective_id=0, has_side_effects=True, vmem_limit_bytes=40 * MIB
@@ -147,19 +163,16 @@
     )(tensor.reshape(rows * slices, columns), factor_j, factor_k)
 
 
-def gram_kernel(count, rows_ref, out_ref, grams, send, recv):
+def exchange(value, count, grams, send, recv):
     me = lax.axis_index("ia")
-    peers = [lax.rem(me + 1 + s, count) for s in range(count - 1)]
-    greet([{"ia": peer} for peer in peers])
-    value = rows_ref[...]
     grams[me] = lax.dot_general(
         value, value, (((0,), (0,)), ((), ())), precision=HIGHEST, preferred_element_type=F32
     )
     copies = []
-    for s, peer in enumerate(peers):
+    for s in range(count - 1):
         copy = pltpu.make_async_remote_copy(
             grams.at[me], grams.at[me], send.at[s], recv.at[s],
-            device_id={"ia": peer}, device_id_type=MESH,
+            device_id={"ia": lax.rem(me + 1 + s, count)}, device_id_type=MESH,
         )
         copy.start()
         copies.append(copy)
@@ -168,9 +181,19 @@
     total = grams[0]
     for index in range(1, count):
         total = total + grams[index]
-    out_ref[...] = total
     for copy in copies:
         copy.wait_send()
+    return total
+
+
+def other_rows(count):
+    me = lax.axis_index("ia")
+    return [{"ia": lax.rem(me + 1 + s, count)} for s in range(count - 1)]
+
+
+def gram_kernel(count, rows_ref, out_ref, grams, send, recv):
+    greet(other_rows(count))
+    out_ref[...] = exchange(rows_ref[...], count, grams, send, recv)
 
 
 def gram_sum(value, count):
@@ -195,32 +218,44 @@
     lines = lax.broadcasted_iota(jnp.int32, (width, width), 0)
     lanes = lax.broadcasted_iota(jnp.int32, (width, width), 1)
     work[:, width:] = jnp.where(lines == lanes, 1.0, 0.0).astype(F32)
+
+    def cell(row, lane):
+        return jnp.broadcast_to(row[:, lane:lane + 1], (1, width))
+
+    def read(first):
+        panel = work[first:first + 8, :]
+        return [[panel[k:k + 1, :width], panel[k:k + 1, width:]] for k in range(8)]
+
+    rows = read(0)
     for first in range(0, width, 8):
-        panel = work[first:first + 8, :]
-        rows = [panel[k:k + 1, :] for k in range(8)]
-        cells = {}
-        for k in range(8):
-            for i in range(k, 8):
-                cells[k, i] = jnp.broadcast_to(
-                    panel[k:k + 1, first + i:first + i + 1], (1, 2 * width)
-                )
+        cells = {(k, i): cell(rows[k][0], first + i) for k in range(8) for i in range(k, 8)}
         for k in range(8):
             scale = lax.rsqrt(cells[k, k])
-            rows[k] = rows[k] * scale
-            lower = [None] * 8
+            rows[k] = [half * scale for half in rows[k]]
+            lower = {i: cells[k, i] * scale for i in range(k + 1, 8)}
             for i in range(k + 1, 8):
-                lower[i] = cells[k, i] * scale
-            for i in range(k + 1, 8):
-                rows[i] = rows[i] - lower[i] * rows[k]
+                rows[i] = [mine - lower[i] * pivot for mine, pivot in zip(rows[i], rows[k])]
                 for m in range(i, 8):
                     cells[i, m] = cells[i, m] - lower[i] * lower[m]
-        done = jnp.concatenate(rows, axis=0)
-        work[first:first + 8, :] = done
+        left = jnp.concatenate([row[0] for row in rows], axis=0)
+        right = jnp.concatenate([row[1] for row in rows], axis=0)
+        work[first:first + 8, :width] = left
+        work[first:first + 8, width:] = right
         if first + 8 < width:
-            work[first + 8:, :] = work[first + 8:, :] - lax.dot_general(
-                done[:, :width], done, (((0,), (0,)), ((), ())),
-                precision=HIGHEST, preferred_element_type=F32,
-            )[first + 8:, :]
+            following = read(first + 8)
+            for i in range(8):
+                for k in range(8):
+                    factor = cell(rows[k][0], first + 8 + i)
+                    following[i] = [
+                        mine - factor * pivot for mine, pivot in zip(following[i], rows[k])
+                    ]
+            if first + 16 < width:
+                done = jnp.concatenate([left, right], axis=1)
+                work[first + 16:, :] = work[first + 16:, :] - lax.dot_general(
+                    left, done, (((0,), (0,)), ((), ())),
+                    precision=HIGHEST, preferred_element_type=F32,
+                )[first + 16:, :]
+            rows = following
 
 
 def apply_kernel(flip, gram_ref, rows_ref, out_ref, work):
@@ -376,8 +411,8 @@
 
 def shards(tensor, factor_j, factor_k):
     count, depth = lax.axis_size("ia"), lax.axis_size("ka")
-    sketch = sketch_sum(tensor, factor_j, factor_k, depth)
-    basis = apply_factor(gram_sum(sketch, count), sketch, False, F32)
+    sketch, gram = sketch_sum(tensor, factor_j, factor_k, count, depth)
+    basis = apply_factor(gram, sketch, False, F32)
     half = apply_factor(gram_sum(basis, count), basis, True, BF16)
     return project(tensor, half, count)
 

time: 117 us -> 106 us (0.906)
  Pallas kernels: 112 us -> 100 us
    pallas_call x2 -> x1, Pallas kernels: 17.8 us -> 9.15 us  [gram_sum(): pl.pallas_call(functools.partial(gram_kernel, count), out_shape=jax.Shape...]
    pallas_call x2, Pallas kernels: 20.6 us -> 14.7 us  [apply_factor(): pl.pallas_call(functools.partial(apply_kernel, flip), out_shape=jax.Shape...]
    pallas_call x1, Pallas kernels: 27.2 us -> 29.4 us  [sketch_sum(): pl.pallas_call(functools.partial(sketch_kernel, count, depth, slices), ou...]
    unnamed x9 -> x11, local copies, waits for them, and re-layouts: 4.78 us -> 5.4 us
where the time goes in v3:
time: 106 us
  Pallas kernels  100 us (94%)
  local copies, waits for them, and re-layouts  5.4 us (5%)
    pallas_call x1, Pallas kernels, project(): pl.pallas_call(functools.partial(project_kernel, count), out_shape=jax.Sh...  47 us
    pallas_call x1, Pallas kernels, sketch_sum(): pl.pallas_call(functools.partial(sketch_kernel, count, depth, slices), ou...  29.4 us
    pallas_call x2, Pallas kernels, apply_factor(): pl.pallas_call(functools.partial(apply_kernel, flip), out_shape=jax.Shape...  14.7 us
    pallas_call x1, Pallas kernels, gram_sum(): pl.pallas_call(functools.partial(gram_kernel, count), out_shape=jax.Shape...  9.15 us
    unnamed x11, local copies, waits for them, and re-layouts  5.4 us

profile of v3, /device:TPU:0, one launch (start us, length us, event | category | flops | bytes accessed | tf_op | source)
XLA Modules:
  0.0 105.6 jit_solution(3288241182948588921)
XLA Ops:
  0.0 0.0 copy-start.1
  0.0 1.0 copy-done.1
  1.0 0.0 copy-start.4
  1.0 0.7 copy-done.4
  1.7 29.4 %shard_map.37 = (f32[1024,128]{1,0:T(8,128)S(1)}, f32[128,128]{1,0:T(8,128)S(1)}) custom-call(bf16[8192,2048]{1,0:T(8,128)(2,1)} %bitcast.1, bf16[2048,128]{1,0:T(8,128)(2,1)S(1)} %copy-done.1, bf16[8,128]{1,0:T(8,128)(2,1)S(1)} %copy-done.4), custom_call_target="tpu_custom_call" | custom-call | flops 4294967296 | bytes 33554432 | tf_op jit(solution)/shard_map/pallas_call | solution.py:136
  31.1 0.0 copy-start.2
  31.1 0.8 copy-done.2
  31.9 0.0 copy-start.3
  31.9 0.6 copy-done.3
  32.5 7.5 %shard_map.38.rows_ref = f32[1024,128]{1,0:T(8,128)} custom-call(f32[128,128]{1,0:T(8,128)} %copy-done.3, f32[1024,128]{1,0:T(8,128)} %copy-done.2), custom_call_target="tpu_custom_call" | custom-call | tf_op jit(solution)/shard_map/pallas_call | solution.py:274
  40.0 9.2 %shard_map.39.gram_ref = f32[128,128]{1,0:T(8,128)} custom-call(f32[1024,128]{1,0:T(8,128)} %shard_map.38.rows_ref), custom_call_target="tpu_custom_call" | custom-call | tf_op jit(solution)/shard_map/pallas_call | solution.py:201
  49.2 7.2 %shard_map.40.half_ref = bf16[128,1024]{1,0:T(8,128)(2,1)} custom-call(f32[128,128]{1,0:T(8,128)} %shard_map.39.gram_ref, f32[1024,128]{1,0:T(8,128)} %shard_map.38.rows_ref), custom_call_target="tpu_custom_call" | custom-call | tf_op jit(solution)/shard_map/pallas_call | solution.py:274
  56.4 0.0 copy-start
  56.4 0.9 copy-done
  57.4 47.0 %shard_map.41 = f32[32,8,2048]{2,1,0:T(8,128)S(1)} custom-call(bf16[8192,2048]{1,0:T(8,128)(2,1)} %bitcast.2, bf16[128,1024]{1,0:T(8,128)(2,1)S(1)} %copy-done), custom_call_target="tpu_custom_call" | custom-call | flops 4294967296 | bytes 33554432 | tf_op jit(solution)/shard_map/pallas_call | solution.py:387
  104.3 1.3 %copy.5 = f32[32,8,2048]{2,1,0:T(8,128)} copy(f32[32,8,2048]{2,1,0:T(8,128)S(1)} %shard_map.41) | data formatting | bytes 4194304
Async XLA Ops:
  0.0 1.0 copy-start.1
  1.0 0.7 copy-start.4
  31.1 0.8 copy-start.2
  31.9 0.6 copy-start.3
  56.4 0.9 copy-start
